TPU v7x, 1024 devices: a whole 4x8x16 slice. The times are simulated.
1024 devices in a mesh: dp: 16 (over y, core), mp: 64 (over z, x).
Axes of the slice: x: 4, y: 8, z: 16, core: 2. Of those that a mesh axis runs over, the one named last changes fastest.
Arguments:
- qkv: bfloat16 [131072, 3840], P(('dp', 'mp')), may hold values from -16 to 16
- send_pos: int32 [16384], P(('dp', 'mp')), may hold values from 0 to 15, as said below
- recv_pos: int32 [16384], P(('dp', 'mp')), may hold values from 0 to 15, as said below
- block_image: int32 [16384], P(('dp', 'mp')), may hold values from 0 to 15, as said below
- owner: int32 [131072, 1], P(('dp', 'mp')), may hold values from 0 to 63; in each aligned block of 128 rows (0 to 127, 128 to 255, ...) at most 3 rows name the same one
- cotangent: bfloat16 [131072, 640], P(('dp', 'mp')), may hold values from -0.109375 to 0.109375
- out_weight: bfloat16 [1280, 1280], replicated, may hold values from -0.15625 to 0.15625
Outputs:
- attended_sent: bfloat16 [196608, 1280], P(('dp', 'mp'))
- grad_out_weight: float32 [409600], P(('dp', 'mp'))
Inputs may be any that keep to these rules, and one draw needn't show every extreme that they name: `send_pos`: within a device the 16 values are distinct; value p + c sends the block to dp index p of the same mp index, slot c. Every device sends exactly 1 block to each of 16 distinct dp indices. `recv_pos`: within a device the 16 values are distinct; value q + c takes the block that dp index q of the same mp index sent in slot c to this device, and that block exists. Every device receives exactly 1 block from each of 16 distinct dp indices. `block_image`: never falls along a device's working blocks and starts at 0 on each device; an image is 1 to 16 blocks; some device holds one image of 16 blocks, and some device holds 16 images of one block each. Of one device's rows, at most 3 have the same owner, and some device has exactly 3 rows for some owner.
All inputs are finite; a program needn't handle non-finite values.
Results may differ from a plain program's by a relative error of at most 0.0057.
Values may be sent and summed in bfloat16 or wider, within the bound.
A program may use at most 32 MiB of HBM per device.

v0:
```python
import math

import jax
import jax.numpy as jnp
from jax import lax
from jax.sharding import PartitionSpec as P

D = 1280
HEADS = 16
HEAD_DIM = 80
BR = 8
NBW = 16


def body(qkv, send_pos, recv_pos, block_image, owner, cotangent, out_weight):
    dp_count = lax.axis_size("dp")
    mp_count = lax.axis_size("mp")
    count, width = qkv.shape
    window = cotangent.shape[1]
    capacity = max(1, NBW // dp_count)
    positions = dp_count * capacity
    block_width = BR * width
    source_blocks = qkv.reshape(NBW, block_width)
    place = (send_pos[None, :] == jnp.arange(positions, dtype=jnp.int32)[:, None]).astype(
        jnp.bfloat16
    )
    outgoing = jnp.dot(place, source_blocks, preferred_element_type=jnp.float32).astype(
        jnp.bfloat16
    )
    incoming = lax.all_to_all(outgoing, "dp", split_axis=0, concat_axis=0, tiled=True)
    select = (recv_pos[:, None] == jnp.arange(positions, dtype=jnp.int32)[None, :]).astype(
        jnp.bfloat16
    )
    packed = jnp.dot(select, incoming, preferred_element_type=jnp.float32).astype(jnp.bfloat16)
    whole = packed.reshape(count, 3, HEADS, HEAD_DIM)
    query = whole[:, 0]
    keys = whole[:, 1]
    values = whole[:, 2]
    scores = jnp.einsum(
        "qhd,khd->hqk", query, keys, preferred_element_type=jnp.float32
    ) / math.sqrt(HEAD_DIM)
    row_image = jnp.repeat(block_image, BR)
    allowed = (row_image[:, None] == row_image[None, :])[None]
    masked = jnp.where(allowed, scores, -jnp.inf)
    highest = jnp.max(masked, axis=-1, keepdims=True)
    weights = jnp.where(allowed, jnp.exp(masked - highest), 0.0)
    probs = (weights / jnp.sum(weights, axis=-1, keepdims=True)).astype(jnp.bfloat16)
    context = jnp.einsum("hqk,khd->qhd", probs, values, preferred_element_type=jnp.float32)
    context = context.reshape(count, D).astype(jnp.bfloat16)
    attended = jnp.dot(context, out_weight, preferred_element_type=jnp.float32).astype(jnp.bfloat16)
    most_rows = 3 * count // (2 * mp_count)
    target = owner[:, 0]
    member = (target[:, None] == jnp.arange(mp_count, dtype=jnp.int32)[None, :]).astype(jnp.int32)
    before = jnp.cumsum(member, axis=0) - member
    rank = jnp.sum(before * member, axis=1)
    position = target * most_rows + rank
    place_rows = (
        position[None, :] == jnp.arange(mp_count * most_rows, dtype=jnp.int32)[:, None]
    ).astype(jnp.bfloat16)
    outgoing_rows = jnp.dot(place_rows, attended, preferred_element_type=jnp.float32).astype(
        jnp.bfloat16
    )
    delivered = lax.all_to_all(
        outgoing_rows.reshape(mp_count, most_rows * D),
        "mp",
        split_axis=0,
        concat_axis=0,
        tiled=True,
    )
    delivered = delivered.reshape(mp_count * most_rows, D)
    context_part = context[:, :window]
    group_rows = lax.psum_scatter(
        jnp.einsum("rd,re->de", context_part, cotangent, preferred_element_type=jnp.float32),
        "dp",
        scatter_dimension=0,
        tiled=True,
    )
    gradient = lax.psum_scatter(group_rows.reshape(-1), "mp", scatter_dimension=0, tiled=True)
    return (delivered, gradient)


def solution(mesh):
    placed = (
        P(("dp", "mp"), None),
        P(("dp", "mp")),
        P(("dp", "mp")),
        P(("dp", "mp")),
        P(("dp", "mp"), None),
        P(("dp", "mp"), None),
        P(),
    )
    return jax.shard_map(
        body,
        mesh=mesh,
        in_specs=placed,
        out_specs=(P(("dp", "mp"), None), P(("dp", "mp"))),
        check_vma=False,
    )
```

profile of v0, /device:TPU:8, one launch (start us, length us, event | category | flops | bytes accessed | tf_op | source)
XLA Modules:
  0.0 440.4 jit_solution(8065961982218021344)
XLA Ops:
  7.2 2.8 reshape.70
  10.0 2.6 fusion.1
  12.5 0.5 broadcast.32
  13.0 3.3 reduce.1
  16.3 2.9 reshape.77
  19.2 17.2 %all-to-all-start = ((bf16[16,2,15360]{2,1,0:T(2,128)(2,1)}), bf16[16,2,15360]{2,1,0:T(2,128)(2,1)}, u32[]{:S(2)}, u32[]{:S(2)}) async-start(bf16[16,2,15360]{2,1,0:T(2,128)(2,1)} %reshape.77), calls=%async_computation | async-start | bytes 1966080 | tf_op jit(solution)/shard_map/all_to_all | solution.py:30
  36.7 23.1 %all-to-all-done = bf16[16,2,15360]{2,1,0:T(2,128)(2,1)} async-done(((bf16[16,2,15360]{2,1,0:T(2,128)(2,1)}), bf16[16,2,15360]{2,1,0:T(2,128)(2,1)}, u32[]{:S(2)}, u32[]{:S(2)}) %all-to-all-start) | async-done | bytes 983072 | tf_op jit(solution)/shard_map/all_to_all | solution.py:30
  59.8 5.6 %reshape.78 = bf16[16,1,30720]{2,1,0:T(2,128)(2,1)} reshape(bf16[16,2,15360]{2,1,0:T(2,128)(2,1)} %all-to-all-done) | data formatting | bytes 1966080
  65.4 3.2 convolution_convert_fusion
  68.7 3.8 reshape.71
  72.5 2.7 fusion.25
  75.1 2.2 copy.32
  77.3 2.2 copy.33
  79.5 2.4 fusion.5
  81.9 1.6 fusion.26
  83.5 2.2 copy.31
  85.7 2.9 convolution_convert_fusion.4
  88.5 2.5 fusion.11
  91.1 0.2 reduce_window_sum.11
  91.5 2.7 convolution_convert_fusion.2
  94.2 3.3 all_to_all.19
  97.5 5.3 %reduce.2 = bf16[64,3840]{1,0:T(8,128)(2,1)} reduce(bf16[64,1,3840]{2,1,0:T(2,128)(2,1)} %all_to_all.19, bf16[]{:T(256)} %broadcast.32), dimensions={1}, to_apply=%all_to_all.19.reduce_sub_computation | reduce | bytes 983042 | tf_op jit(solution)/shard_map/all_to_all | solution.py:63
  102.9 1.9 reshape.79
  104.8 12.9 %all-to-all-start.1 = ((bf16[64,2,1920]{2,1,0:T(2,128)(2,1)}), bf16[64,2,1920]{2,1,0:T(2,128)(2,1)}, u32[]{:S(2)}, u32[]{:S(2)}) async-start(bf16[64,2,1920]{2,1,0:T(2,128)(2,1)} %reshape.79), calls=%async_computation.1 | async-start | bytes 983040 | tf_op jit(solution)/shard_map/all_to_all | solution.py:63
  117.7 34.9 %reduce-scatter.4.cloned.1.call-done = f32[40,640]{1,0:T(8,128)} async-done(((f32[640,640]{1,0:T(8,128)}), f32[40,640]{1,0:T(8,128)}) %reduce-scatter.4.cloned.1.call-update) | async-done | bytes 102416
  152.6 1.5 reshape.73
  154.2 1.3 dynamic-slice.2
  156.1 3.4 reshape.80
  159.5 4.7 %reduce = bf16[64,3840]{1,0:T(8,128)(2,1)} reduce(bf16[64,1,3840]{2,1,0:T(2,128)(2,1)} %reshape.80, bf16[]{:T(256)} %constant.29), dimensions={1}, to_apply=%all_to_all.18.reduce_sub_computation | reduce | bytes 983042 | tf_op jit(solution)/shard_map/all_to_all | solution.py:63
  164.2 2.0 reshape.72
  166.2 266.0 %all-reduce.4.cloned.1.call-done = f32[25600]{0:T(1024)} async-done(((f32[25600]{0:T(1024)}), f32[25600]{0:T(1024)}) %all-reduce.4.cloned.1.call-update) | async-done | bytes 102416
  432.2 1.3 dynamic-slice.3
  (23 shorter events, 0.7 us)
Async XLA Ops:
  7.2 84.3 %copy-start = (bf16[1280,1280]{1,0:T(8,128)(2,1)S(1)}, bf16[1280,1280]{1,0:T(8,128)(2,1)}, u32[]{:S(2)}) copy-start(bf16[1280,1280]{1,0:T(8,128)(2,1)} %param.13) | copy-start | bytes 9830404
  7.2 2.8 copy-start.3
  16.3 20.1 %copy-start.5 = (s32[16]{0:T(128)S(1)}, s32[16]{0:T(128)}, u32[]{:S(2)}) copy-start(s32[16]{0:T(128)} %param.10) | copy-start | bytes 196
  19.2 40.6 %all-to-all-start = ((bf16[16,2,15360]{2,1,0:T(2,128)(2,1)}), bf16[16,2,15360]{2,1,0:T(2,128)(2,1)}, u32[]{:S(2)}, u32[]{:S(2)}) async-start(bf16[16,2,15360]{2,1,0:T(2,128)(2,1)} %reshape.77), calls=%async_computation | async-start | bytes 1966080 | tf_op jit(solution)/shard_map/all_to_all | solution.py:30
  36.4 29.1 %copy-start.4 = (s32[16]{0:T(128)S(1)}, s32[16]{0:T(128)}, u32[]{:S(2)}) copy-start(s32[16]{0:T(128)} %param.9) | copy-start | bytes 196
  36.4 116.2 %reduce-scatter.4.cloned.1.call-start = ((), (), s32[]{:S(2)}) async-start(), calls=%async_computation.4 | async-start | bytes 1740800
  85.7 2.9 copy-start.1
  88.5 2.5 copy-start.2
  104.8 51.3 %all-to-all-start.1 = ((bf16[64,2,1920]{2,1,0:T(2,128)(2,1)}), bf16[64,2,1920]{2,1,0:T(2,128)(2,1)}, u32[]{:S(2)}, u32[]{:S(2)}) async-start(bf16[64,2,1920]{2,1,0:T(2,128)(2,1)} %reshape.79), calls=%async_computation.1 | async-start | bytes 983040 | tf_op jit(solution)/shard_map/all_to_all | solution.py:63
  117.7 314.5 %all-reduce.4.cloned.1.call-start = ((), (), s32[]{:S(2)}) async-start(), calls=%async_computation.3 | async-start | bytes 204800
Sparse Core Ops, SparseCore 0:
  91.2 61.3 reduce-scatter.3
  156.4 275.7 all-reduce.3
where the time goes:
time: 442 us; the launch traced here: 440 us
  waiting for transfers between devices  324 us (73%)
  local copies, waits for them, and re-layouts  39.8 us (9%)
  starting transfers between devices  30.1 us (7%)
  matrix products  17.9 us (4%)
  between operations  14.8 us (3%)
  other arithmetic  13.8 us (3%)
    unnamed x4, waiting for transfers between devices  301 us
    all_to_all x1, waiting for transfers between devices, body(): lax.all_to_all(outgoing, 'dp', split_axis=0, concat_axis=0, tiled=True)  23.1 us
    unnamed x21, local copies, waits for them, and re-layouts  23 us
    all_to_all x1, starting transfers between devices, body(): lax.all_to_all(outgoing, 'dp', split_axis=0, concat_axis=0, tiled=True)  17.2 us
    all_to_all x1, starting transfers between devices, body(): lax.all_to_all(outgoing_rows.reshape(mp_count, most_rows * D), 'mp', spli...  12.9 us
    all_to_all x2, other arithmetic, body(): lax.all_to_all(outgoing_rows.reshape(mp_count, most_rows * D), 'mp', spli...  10 us
  transfers between devices with their start and end apart: 4, of which 3 were waited for; matrix products, arithmetic and copies ran while one was open for 5% of the time, Pallas kernels for 0%

commit v1 on v0

v1 whole, which is shorter than its diff:
```python
import functools
import math

import jax
import jax.numpy as jnp
from jax import lax
from jax.experimental import pallas as pl
from jax.experimental.pallas import tpu as pltpu
from jax.sharding import PartitionSpec as P

MESH = pl.DeviceIdType.MESH
D = 1280
HEAD = 80
GW = 640
BR = 8
NX = 4
CHUNKS = 4
HPC = 4
CC = HPC * HEAD
TILES = ((0, 1, 2), (3, 4), (5, 6, 7), (8, 9))
WIDTHS = tuple(3 * 128 * len(t) for t in TILES)
STARTS = tuple(sum(WIDTHS[:c]) for c in range(CHUNKS))
AROWS = 128
PIECE = 400
PADDED = 512
F32 = jnp.float32
BF16 = jnp.bfloat16


def place_of(kind, tile):
    for c, tiles in enumerate(TILES):
        if tile in tiles:
            return STARTS[c] + 128 * (kind * len(tiles) + tiles.index(tile))
    raise ValueError


def kernel(
    ndp,
    nz,
    send_ref,
    take_ref,
    image_ref,
    owner_ref,
    qkv_hbm,
    cot_hbm,
    w_hbm,
    out_ref,
    grad_ref,
    qkv_v,
    cot_v,
    wpad,
    stage,
    recv,
    packed,
    bias,
    pcat,
    rhs,
    zsend,
    zrecv,
    fin,
    unpack,
    acc,
    inter,
    gcot,
    gctx,
    edge,
    gbuf,
    gdp_send,
    gdp_recv,
    gz_send,
    gz_recv,
    source_of,
    work_of,
    local_sem,
    y_send,
    y_recv,
    z_send,
    z_recv,
    x_send,
    x_recv,
    g_send,
    g_recv,
):
    p = lax.axis_index("dp")
    j = lax.axis_index("mp")
    z = lax.div(j, NX)
    x = lax.rem(j, NX)
    nb = ndp
    rows = nb * BR
    nmp = nz * NX
    arows = AROWS // ndp
    per_z = 2 * arows // nz

    def dp_peer(i):
        return lax.rem(p + i, ndp)

    def z_peer(i):
        return lax.rem(z + i, nz)

    def x_peer(i):
        return lax.rem(x + i, NX)

    qkv_copy = pltpu.make_async_copy(qkv_hbm, qkv_v, local_sem.at[0])
    cot_copy = pltpu.make_async_copy(cot_hbm, cot_v, local_sem.at[1])
    w_copy = pltpu.make_async_copy(w_hbm, wpad.at[pl.ds(64, D)], local_sem.at[2])
    qkv_copy.start()
    cot_copy.start()

    barrier = pltpu.get_barrier_semaphore()

    @pl.loop(1, ndp)
    def _(i):
        pl.semaphore_signal(barrier, inc=1, device_id=(dp_peer(i), j), device_id_type=MESH)

    @pl.loop(1, nz)
    def _(i):
        pl.semaphore_signal(barrier, inc=1, device_id=(p, z_peer(i) * NX + x), device_id_type=MESH)

    @pl.loop(1, NX)
    def _(i):
        pl.semaphore_signal(barrier, inc=1, device_id=(p, z * NX + x_peer(i)), device_id_type=MESH)

    @pl.loop(0, nb)
    def _(v):
        source, work = jnp.int32(0), jnp.int32(0)
        for s in range(nb):
            source = jnp.where(send_ref[s] == v, s, source)
            work = jnp.where(take_ref[s] == v, s, work)
        source_of[v] = source
        work_of[v] = work

    qkv_copy.wait()
    w_copy.start()
    pl.semaphore_wait(barrier, ndp + nz + NX - 3)

    def block_of(target, c):
        s = source_of[target]
        first, many = TILES[c][0] * 128, 128 * len(TILES[c])
        return [qkv_v[s, :, kind * D + first : kind * D + first + many] for kind in range(3)]

    def y_copy(c, target):
        columns = pl.ds(STARTS[c], WIDTHS[c])
        return pltpu.make_async_remote_copy(
            src_ref=stage.at[target, :, columns],
            dst_ref=recv.at[p, :, columns],
            send_sem=y_send.at[c],
            recv_sem=y_recv.at[c],
            device_id=(target, j),
            device_id_type=MESH,
        )

    def send_chunk(c):
        many = WIDTHS[c] // 3

        @pl.loop(1, ndp)
        def _(i):
            target = dp_peer(i)
            for kind, part in enumerate(block_of(target, c)):
                stage[target, :, STARTS[c] + kind * many : STARTS[c] + (kind + 1) * many] = part
            y_copy(c, target).start()

        for kind, part in enumerate(block_of(p, c)):
            recv[p, :, STARTS[c] + kind * many : STARTS[c] + (kind + 1) * many] = part

    send_chunk(0)

    cot_copy.wait()

    @pl.loop(0, nb // 2)
    def _(i):
        pair = [cot_v[work_of[2 * i + b]].astype(F32) for b in range(2)]
        gcot[x, pl.ds(pl.multiple_of(2 * BR * i, 2 * BR), 2 * BR), :] = jnp.concatenate(pair, axis=0).astype(BF16)

    def x_gather(buffer, which, target):
        return pltpu.make_async_remote_copy(
            src_ref=buffer.at[x],
            dst_ref=buffer.at[x],
            send_sem=g_send.at[which],
            recv_sem=g_recv.at[which],
            device_id=(p, z * NX + target),
            device_id_type=MESH,
        )

    @pl.loop(1, NX)
    def _(i):
        x_gather(gcot, 0, x_peer(i)).start()

    for c in range(1, CHUNKS):
        send_chunk(c)

    wpad[0:64, :] = jnp.zeros((64, D), BF16)
    wpad[64 + D : 128 + D, :] = jnp.zeros((64, D), BF16)
    acc[...] = jnp.zeros_like(acc)

    row = lax.broadcasted_iota(jnp.int32, (rows, rows), 0)
    lane = lax.broadcasted_iota(jnp.int32, (rows, rows), 1)
    image_row = jnp.zeros((rows, rows), jnp.int32)
    image_lane = jnp.zeros((rows, rows), jnp.int32)
    slot_row = jnp.zeros((rows, rows), jnp.int32)
    for v in range(nb):
        image = image_ref[work_of[v]]
        image_row = jnp.where(lax.div(row, BR) == v, image, image_row)
        image_lane = jnp.where(lax.div(lane, BR) == v, image, image_lane)
        slot_row = jnp.where(lax.div(row, BR) == v, take_ref[v], slot_row)
    bias[...] = jnp.where(image_row == image_lane, 0.0, -jnp.inf)

    to_slot = jnp.where(
        (slot_row == lax.div(lane, BR)) & (lax.rem(row, BR) == lax.rem(lane, BR)), 1.0, 0.0
    ).astype(BF16)
    target_lane = jnp.broadcast_to(owner_ref[...], (rows, rows)).astype(F32)
    target_row = jnp.transpose(target_lane)
    earlier = jnp.where((target_row == target_lane) & (row < lane), 1.0, 0.0)
    rank = jnp.sum(earlier, axis=0, keepdims=True)
    code_work = target_lane[0:1, :] * 4.0 + rank
    code = jnp.dot(jnp.broadcast_to(code_work, (16, rows)).astype(BF16), to_slot, preferred_element_type=F32)
    line = lax.broadcasted_iota(jnp.int32, (nmp * 8, rows), 0)
    part = lax.rem(line, 8)
    base = lax.div(line, 8) * 4
    code_a = jnp.where(part <= 2, base, jnp.where(part >= 5, base + 2, -1)).astype(F32)
    code_b = jnp.where((part >= 2) & (part <= 4), base + 1, -1).astype(F32)
    code_all = jnp.broadcast_to(code[0:1, :], (nmp * 8, rows))
    pcat[:, 0:rows] = jnp.where(code_a == code_all, 1.0, 0.0).astype(BF16)
    pcat[:, rows : 2 * rows] = jnp.where(code_b == code_all, 1.0, 0.0).astype(BF16)

    def tile(kind, t):
        start = place_of(kind, t)
        return packed[:, start : start + 128]

    def attend(c):
        columns = pl.ds(STARTS[c], WIDTHS[c])
        arrived = recv.at[pl.ds(0, ndp - 1), :, columns]
        pltpu.make_async_copy(arrived, arrived, y_recv.at[c]).wait()
        mine = slice(STARTS[c], STARTS[c] + WIDTHS[c])
        packed[:, mine] = recv[:, :, mine].astype(F32).reshape(rows, WIDTHS[c]).astype(BF16)
        first = c * CC // 128
        tiles = [jnp.zeros((rows, 128), F32) for _ in range(3)]
        column = lax.broadcasted_iota(jnp.int32, (rows, 128), 1)
        for h in range(c * HPC, (c + 1) * HPC):
            low = h * HEAD
            span = range(low // 128, (low + HEAD - 1) // 128 + 1)
            inside = [(column + 128 * t >= low) & (column + 128 * t < low + HEAD) for t in span]
            query = [tile(0, t) * jnp.where(m, 1.0, 0.0).astype(BF16) for t, m in zip(span, inside)]
            query = jnp.concatenate(query, axis=1) if len(query) > 1 else query[0]
            keys = [tile(1, t) for t in span]
            keys = jnp.concatenate(keys, axis=1) if len(keys) > 1 else keys[0]
            values = [tile(2, t) for t in span]
            values = jnp.concatenate(values, axis=1) if len(values) > 1 else values[0]
            scores = lax.dot_general(query, keys, (((1,), (1,)), ((), ())), preferred_element_type=F32)
            scores = scores * (1.0 / math.sqrt(HEAD)) + bias[...]
            weights = jnp.exp(scores - jnp.max(scores, axis=-1, keepdims=True))
            probs = (weights / jnp.sum(weights, axis=-1, keepdims=True)).astype(BF16)
            context = jnp.dot(probs, values, preferred_element_type=F32)
            for i, (t, m) in enumerate(zip(span, inside)):
                tiles[t - first] = jnp.where(m, context[:, 128 * i : 128 * i + 128], tiles[t - first])
        natural = jnp.concatenate(tiles, axis=1).astype(BF16)
        if c == 0:
            gctx[x, :, 0:256] = natural[:, 0:256]
            edge[...] = natural[:, 256:384]
        if c == 1:
            gctx[x, :, 256:384] = natural[:, 0:128] + edge[...]
            gctx[x, :, 384:640] = natural[:, 128:384]
        turned = pltpu.roll(natural.astype(F32), 64 if c % 2 == 0 else 384 - 64, axis=1).astype(BF16)
        a, b = (natural, turned) if c % 2 == 0 else (turned, natural)
        rhs[0:rows, :] = a
        rhs[rows : 2 * rows, 0:256] = b[:, 128:384]
        rhs[rows : 2 * rows, 256:384] = b[:, 0:128]
        placed = jnp.dot(pcat[...], rhs[...], preferred_element_type=F32)
        kind = lax.rem(lax.broadcasted_iota(jnp.int32, (nmp * 8, 128), 0), 8)
        zero = (kind == 0) | (kind == 3) | (kind == 5)
        one = (kind == 1) | (kind == 4) | (kind == 6)
        chosen = jnp.where(zero, placed[:, 0:128], jnp.where(one, placed[:, 128:256], placed[:, 256:384]))
        zsend[c] = chosen.reshape(nz, NX, 8, 128).astype(BF16)

        @pl.loop(1, nz)
        def _(i):
            z_copy(c, z_peer(i)).start()

        zrecv[c, z] = zsend[c, z]

    def z_copy(c, target):
        return pltpu.make_async_remote_copy(
            src_ref=zsend.at[c, target],
            dst_ref=zrecv.at[c, z],
            send_sem=z_send.at[c],
            recv_sem=z_recv.at[c],
            device_id=(p, target * NX + x),
            device_id_type=MESH,
        )

    def x_copy(c, target):
        return pltpu.make_async_remote_copy(
            src_ref=zrecv.at[c, :, target],
            dst_ref=fin.at[c, :, x],
            send_sem=x_send.at[c],
            recv_sem=x_recv.at[c],
            device_id=(p, z * NX + target),
            device_id_type=MESH,
        )

    def relay(c):
        arrived = zrecv.at[c, pl.ds(0, nz - 1)]
        pltpu.make_async_copy(arrived, arrived, z_recv.at[c]).wait()

        @pl.loop(1, NX)
        def _(i):
            x_copy(c, x_peer(i)).start()

        fin[c, :, x] = zrecv[c, :, x]

    def project(c):
        arrived = fin.at[c, :, pl.ds(0, NX - 1)]
        pltpu.make_async_copy(arrived, arrived, x_recv.at[c]).wait()
        unpack[...] = fin[c].astype(F32).reshape(nmp * 8, 128)
        s = [unpack[pl.ds(i, nmp, stride=8), :] for i in range(8)]
        low = lax.broadcasted_iota(jnp.int32, (nmp, 128), 1) < 64
        zeroth = jnp.concatenate([s[0], s[1], jnp.where(low, s[2], 0.0)], axis=1)
        second = jnp.concatenate([s[5], s[6], s[7]], axis=1)
        first = jnp.concatenate([jnp.where(low, 0.0, s[2]), s[3], s[4]], axis=1).astype(BF16)
        both = jnp.concatenate([zeroth, second], axis=0).astype(BF16)
        start = c * CC
        acc[0 : 2 * nmp, :] += jnp.dot(both, wpad[start + 64 : start + 448, :], preferred_element_type=F32)
        acc[2 * nmp : 3 * nmp, :] += jnp.dot(first, wpad[start : start + 384, :], preferred_element_type=F32)

    def gdp_copy(target):
        return pltpu.make_async_remote_copy(
            src_ref=gdp_send.at[target],
            dst_ref=gdp_recv.at[p],
            send_sem=g_send.at[2],
            recv_sem=g_recv.at[2],
            device_id=(target, j),
            device_id_type=MESH,
        )

    def gz_copy(target):
        return pltpu.make_async_remote_copy(
            src_ref=gz_send.at[target],
            dst_ref=gz_recv.at[z],
            send_sem=g_send.at[3],
            recv_sem=g_recv.at[3],
            device_id=(p, target * NX + x),
            device_id_type=MESH,
        )

    def send_context():
        @pl.loop(1, NX)
        def _(i):
            x_gather(gctx, 1, x_peer(i)).start()

    def gradient_product():
        for which, buffer in ((0, gcot), (1, gctx)):
            arrived = buffer.at[pl.ds(0, NX - 1)]
            pltpu.make_async_copy(arrived, arrived, g_recv.at[which]).wait()
        right = gcot[...].reshape(NX * rows, GW)
        for m in range(GW // 128):
            left = gctx[:, :, 128 * m : 128 * m + 128].reshape(NX * rows, 128)
            product = lax.dot_general(left, right, (((0,), (0,)), ((), ())), preferred_element_type=F32)
            for t in range(GW // 128):
                gbuf[t, 128 * m : 128 * m + 128, :] = product[:, 128 * t : 128 * t + 128]
        for k in range(NX):

            @pl.when(x == k)
            def _():
                for half in range(2):
                    start = 1600 * half + PIECE * k
                    tiles = [min(start // 128 + i, 24) for i in range(5)]
                    flat = [gbuf[t % 5, pl.ds(t // 5, AROWS, stride=5), :] for t in tiles]
                    flat = jnp.concatenate(flat, axis=1)
                    if start % 128:
                        flat = pltpu.roll(flat, 640 - start % 128, axis=1)
                    flat = flat[:, 0:PADDED].reshape(ndp, arows, PADDED).astype(BF16)
                    gdp_send[:, :, half * PADDED : (half + 1) * PADDED] = flat

        @pl.loop(1, ndp)
        def _(i):
            gdp_copy(dp_peer(i)).start()

        gdp_recv[p] = gdp_send[p]

    def gradient_over_dp():
        arrived = gdp_recv.at[pl.ds(0, ndp - 1)]
        pltpu.make_async_copy(arrived, arrived, g_recv.at[2]).wait()
        total = gdp_recv[0].astype(F32)
        for i in range(1, ndp):
            total = total + gdp_recv[i].astype(F32)
        for a in range(arows):
            for half in range(2):
                n = 2 * a + half
                gz_send[n // per_z, n % per_z : n % per_z + 1, :] = total[a : a + 1, half * PADDED : (half + 1) * PADDED]

        @pl.loop(1, nz)
        def _(i):
            gz_copy(z_peer(i)).start()

        gz_recv[z] = gz_send[z]

    def gradient_over_z():
        arrived = gz_recv.at[pl.ds(0, nz - 1)]
        pltpu.make_async_copy(arrived, arrived, g_recv.at[3]).wait()
        total = gz_recv[0]
        for i in range(1, nz):
            total = total + gz_recv[i]
        grad_ref[...] = total

    attend(0)
    attend(1)
    send_context()
    relay(0)
    attend(2)
    w_copy.wait()
    relay(1)
    gradient_product()
    project(0)
    attend(3)
    relay(2)
    project(1)
    gradient_over_dp()
    project(2)
    relay(3)
    gradient_over_z()
    project(3)

    for t in range(D // 128):
        for k, start in ((0, 0), (2, nmp), (1, 2 * nmp)):
            inter[t, pl.ds(k, nmp, stride=3), :] = acc[start : start + nmp, 128 * t : 128 * t + 128]
        out_ref[:, 128 * t : 128 * t + 128] = inter[t].astype(BF16)

    for c in range(CHUNKS):
        gone = stage.at[pl.ds(0, ndp - 1), :, pl.ds(STARTS[c], WIDTHS[c])]
        pltpu.make_async_copy(gone, gone, y_send.at[c]).wait()
        gone = zsend.at[c, pl.ds(0, nz - 1)]
        pltpu.make_async_copy(gone, gone, z_send.at[c]).wait()
        gone = zrecv.at[c, :, pl.ds(0, NX - 1)]
        pltpu.make_async_copy(gone, gone, x_send.at[c]).wait()
    for which, buffer, many in ((0, gcot, NX), (1, gctx, NX), (2, gdp_send, ndp), (3, gz_send, nz)):
        gone = buffer.at[pl.ds(0, many - 1)]
        pltpu.make_async_copy(gone, gone, g_send.at[which]).wait()


def solution(mesh):
    ndp, nmp = mesh.shape["dp"], mesh.shape["mp"]
    nz = nmp // NX
    nb = ndp
    rows = nb * BR
    arows = AROWS // ndp
    per_z = 2 * arows // nz

    def body(qkv, send_pos, recv_pos, block_image, owner, cotangent, out_weight):
        smem = pl.BlockSpec(memory_space=pltpu.SMEM)
        vmem = pl.BlockSpec(memory_space=pltpu.VMEM)
        hbm = pl.BlockSpec(memory_space=pl.ANY)
        delivered, gradient = pl.pallas_call(
            functools.partial(kernel, ndp, nz),
            out_shape=(
                jax.ShapeDtypeStruct((3 * nmp, D), BF16),
                jax.ShapeDtypeStruct((per_z, PADDED), F32),
            ),
            in_specs=[smem, smem, smem, vmem, hbm, hbm, hbm],
            out_specs=(vmem, vmem),
            scratch_shapes=[
                pltpu.VMEM((nb, BR, 3 * D), BF16),
                pltpu.VMEM((nb, BR, GW), BF16),
                pltpu.VMEM((D + 128, D), BF16),
                pltpu.VMEM((nb, BR, 3 * D), BF16),
                pltpu.VMEM((nb, BR, 3 * D), BF16),
                pltpu.VMEM((rows, 3 * D), BF16),
                pltpu.VMEM((rows, rows), F32),
                pltpu.VMEM((nmp * 8, 2 * rows), BF16),
                pltpu.VMEM((2 * rows, 384), BF16),
                pltpu.VMEM((CHUNKS, nz, NX, 8, 128), BF16),
                pltpu.VMEM((CHUNKS, nz, NX, 8, 128), BF16),
                pltpu.VMEM((CHUNKS, nz, NX, 8, 128), BF16),
                pltpu.VMEM((nmp * 8, 128), F32),
                pltpu.VMEM((3 * nmp, D), F32),
                pltpu.VMEM((D // 128, 3 * nmp, 128), F32),
                pltpu.VMEM((NX, rows, GW), BF16),
                pltpu.VMEM((NX, rows, GW), BF16),
                pltpu.VMEM((rows, 128), BF16),
                pltpu.VMEM((GW // 128, GW, 128), F32),
                pltpu.VMEM((ndp, arows, 2 * PADDED), BF16),
                pltpu.VMEM((ndp, arows, 2 * PADDED), BF16),
                pltpu.VMEM((nz, per_z, PADDED), F32),
                pltpu.VMEM((nz, per_z, PADDED), F32),
                pltpu.SMEM((nb,), jnp.int32),
                pltpu.SMEM((nb,), jnp.int32),
                pltpu.SemaphoreType.DMA((3,)),
                pltpu.SemaphoreType.DMA((CHUNKS,)),
                pltpu.SemaphoreType.DMA((CHUNKS,)),
                pltpu.SemaphoreType.DMA((CHUNKS,)),
                pltpu.SemaphoreType.DMA((CHUNKS,)),
                pltpu.SemaphoreType.DMA((CHUNKS,)),
                pltpu.SemaphoreType.DMA((CHUNKS,)),
                pltpu.SemaphoreType.DMA((4,)),
                pltpu.SemaphoreType.DMA((4,)),
            ],
            compiler_params=pltpu.CompilerParams(
                collective_id=0, has_side_effects=True, vmem_limit_bytes=40 * 2**20
            ),
        )(
            send_pos,
            recv_pos,
            block_image,
            owner.reshape(1, rows),
            qkv.reshape(nb, BR, 3 * D),
            cotangent.reshape(nb, BR, GW),
            out_weight,
        )
        return delivered, gradient[:, :PIECE].reshape(-1)

    placed = (
        P(("dp", "mp"), None),
        P(("dp", "mp")),
        P(("dp", "mp")),
        P(("dp", "mp")),
        P(("dp", "mp"), None),
        P(("dp", "mp"), None),
        P(),
    )
    return jax.shard_map(
        body,
        mesh=mesh,
        in_specs=placed,
        out_specs=(P(("dp", "mp"), None), P(("dp", "mp"))),
        check_vma=False,
    )
```

time: 442 us -> 81.9 us (0.19)
  the two profiles are of different devices: /device:TPU:8 before, /device:TPU:1 now
where the time goes in v1:
time: 81.9 us; the launch traced here: 81.7 us
  Pallas kernels  73 us (89%)
  local copies, waits for them, and re-layouts  8.01 us (10%)
    pallas_call x1, Pallas kernels, body(): pl.pallas_call(functools.partial(kernel, ndp, nz), out_shape=(jax.ShapeDt...  73 us
    unnamed x16, local copies, waits for them, and re-layouts  8.01 us

profile of v1, /device:TPU:1, one launch (start us, length us, event | category | flops | bytes accessed | tf_op | source)
XLA Modules:
  0.0 81.7 jit_solution(7734339688881136261)
XLA Ops:
  0.6 0.0 copy-start
  0.6 1.9 %copy-done = bf16[1280,1280]{1,0:T(8,128)(2,1)S(1)} copy-done((bf16[1280,1280]{1,0:T(8,128)(2,1)S(1)}, bf16[1280,1280]{1,0:T(8,128)(2,1)}, u32[]{:S(2)}) %copy-start) | copy-done | bytes 3276824
  2.6 0.0 copy-start.1
  2.6 1.2 %copy-done.1 = bf16[128,3840]{1,0:T(8,128)(2,1)S(1)} copy-done((bf16[128,3840]{1,0:T(8,128)(2,1)S(1)}, bf16[128,3840]{1,0:T(8,128)(2,1)}, u32[]{:S(2)}) %copy-start.1) | copy-done | bytes 983064
  3.8 0.0 copy-start.2
  3.8 0.9 %copy-done.2 = bf16[128,640]{1,0:T(8,128)(2,1)S(1)} copy-done((bf16[128,640]{1,0:T(8,128)(2,1)S(1)}, bf16[128,640]{1,0:T(8,128)(2,1)}, u32[]{:S(2)}) %copy-start.2) | copy-done | bytes 163864
  4.7 0.0 copy-start.3
  4.7 0.7 copy-done.3
  5.3 0.0 copy-start.4
  5.3 0.7 copy-done.4
  6.0 0.0 copy-start.5
  6.0 0.7 copy-done.5
  6.6 0.0 copy-start.6
  6.6 0.7 copy-done.6
  7.3 73.0 %shard_map.86 = (bf16[192,1280]{1,0:T(8,128)(2,1)S(1)}, f32[1,512]{1,0:T(1,128)S(1)}) custom-call(s32[16]{0:T(128)S(1)} %copy-done.3, s32[16]{0:T(128)S(1)} %copy-done.4, s32[16]{0:T(128)S(1)} %copy-done.5, s32[1,128]{1,0:T(1,128)S(1)} %bitcast.8, bf16[16,8,3840]{2,1,0:T(8,128)(2,1)S(1)} %bitcast.5, bf16[16,8,640]{2,1,0:T(8,128)(2,1)S(1)} %bitcast.6, ...), custom_call_target="tpu_custom_call" | custom-call | tf_op jit(solution)/shard_map/pallas_call | solution.py:451
  80.3 0.8 copy.11
  81.1 0.6 copy.12
Async XLA Ops:
  0.6 1.9 %copy-start = (bf16[1280,1280]{1,0:T(8,128)(2,1)S(1)}, bf16[1280,1280]{1,0:T(8,128)(2,1)}, u32[]{:S(2)}) copy-start(bf16[1280,1280]{1,0:T(8,128)(2,1)} %w_hbm.1) | copy-start | bytes 9830404
  2.6 1.2 %copy-start.1 = (bf16[128,3840]{1,0:T(8,128)(2,1)S(1)}, bf16[128,3840]{1,0:T(8,128)(2,1)}, u32[]{:S(2)}) copy-start(bf16[128,3840]{1,0:T(8,128)(2,1)} %param.7) | copy-start | bytes 2949124
  3.8 0.9 %copy-start.2 = (bf16[128,640]{1,0:T(8,128)(2,1)S(1)}, bf16[128,640]{1,0:T(8,128)(2,1)}, u32[]{:S(2)}) copy-start(bf16[128,640]{1,0:T(8,128)(2,1)} %param.12) | copy-start | bytes 491524
  4.7 0.7 copy-start.3
  5.3 0.7 copy-start.4
  6.0 0.7 copy-start.5
  6.6 0.7 copy-start.6

commit v2 on v1

--- a/solution.py
+++ b/solution.py
@@ -91,11 +91,14 @@
     arows = AROWS // ndp
     per_z = 2 * arows // nz
 
+    def offset(i, n):
+        return jnp.where(lax.rem(i, 2) == 1, n // 2 - lax.div(i, 2), n - n // 2 + lax.div(i, 2))
+
     def dp_peer(i):
-        return lax.rem(p + i, ndp)
+        return lax.rem(p + offset(i, ndp), ndp)
 
     def z_peer(i):
-        return lax.rem(z + i, nz)
+        return lax.rem(z + offset(i, nz), nz)
 
     def x_peer(i):
         return lax.rem(x + i, NX)
@@ -230,6 +233,8 @@
         columns = pl.ds(STARTS[c], WIDTHS[c])
         arrived = recv.at[pl.ds(0, ndp - 1), :, columns]
         pltpu.make_async_copy(arrived, arrived, y_recv.at[c]).wait()
+        if c == CHUNKS - 1:
+            send_gradient()
         mine = slice(STARTS[c], STARTS[c] + WIDTHS[c])
         packed[:, mine] = recv[:, :, mine].astype(F32).reshape(rows, WIDTHS[c]).astype(BF16)
         first = c * CC // 128
@@ -370,11 +375,12 @@
                     flat = flat[:, 0:PADDED].reshape(ndp, arows, PADDED).astype(BF16)
                     gdp_send[:, :, half * PADDED : (half + 1) * PADDED] = flat
 
+        gdp_recv[p] = gdp_send[p]
+
+    def send_gradient():
         @pl.loop(1, ndp)
         def _(i):
             gdp_copy(dp_peer(i)).start()
-
-        gdp_recv[p] = gdp_send[p]
 
     def gradient_over_dp():
         arrived = gdp_recv.at[pl.ds(0, ndp - 1)]
@@ -493,7 +499,7 @@
                 pltpu.SemaphoreType.DMA((4,)),
             ],
             compiler_params=pltpu.CompilerParams(
-                collective_id=0, has_side_effects=True, vmem_limit_bytes=40 * 2**20
+                collective_id=0, has_side_effects=True, vmem_limit_bytes=62 * 2**20
             ),
         )(
             send_pos,

time: 81.9 us -> 72.3 us (0.88)
  local copies, waits for them, and re-layouts: 8.01 us -> 3.08 us
  Pallas kernels: 73 us -> 68.3 us
    unnamed x16 -> x2, local copies, waits for them, and re-layouts: 8.01 us -> 3.08 us
    pallas_call x1, Pallas kernels: 73 us -> 68.3 us  [body(): pl.pallas_call(functools.partial(kernel, ndp, nz), out_shape=(jax.ShapeDt...]
where the time goes in v2:
time: 72.3 us; the launch traced here: 72 us
  Pallas kernels  68.3 us (94%)
  local copies, waits for them, and re-layouts  3.08 us (4%)
    pallas_call x1, Pallas kernels, body(): pl.pallas_call(functools.partial(kernel, ndp, nz), out_shape=(jax.ShapeDt...  68.3 us
    unnamed x2, local copies, waits for them, and re-layouts  3.08 us

profile of v2, /device:TPU:1, one launch (start us, length us, event | category | flops | bytes accessed | tf_op | source)
XLA Modules:
  0.0 72.0 jit_solution(8977691695438116087)
XLA Ops:
  0.6 68.3 %shard_map.86 = (bf16[192,1280]{1,0:T(8,128)(2,1)}, f32[1,512]{1,0:T(1,128)}) custom-call(s32[16]{0:T(128)} %send_ref.1, s32[16]{0:T(128)} %take_ref.1, s32[16]{0:T(128)} %image_ref.1, s32[1,128]{1,0:T(1,128)} %bitcast.8, bf16[16,8,3840]{2,1,0:T(8,128)(2,1)} %bitcast.5, bf16[16,8,640]{2,1,0:T(8,128)(2,1)} %bitcast.6, bf16[1280,1280]{1,0:T(8,128)(2,1)} %w_hbm.1), custom_call_target="tpu_custom_call" | custom-call | tf_op jit(solution)/shard_map/pallas_call | solution.py:457
  68.9 1.8 %copy.11 = bf16[192,1280]{1,0:T(8,128)(2,1)} copy(bf16[192,1280]{1,0:T(8,128)(2,1)} %get-tuple-element.8) | data formatting | bytes 983040
  70.8 1.2 %copy.12 = f32[400]{0:T(512)} copy(f32[400]{0:T(512)} %bitcast.7) | data formatting | bytes 3200

commit v3 on v2

--- a/solution.py
+++ b/solution.py
@@ -37,10 +37,10 @@
 def kernel(
     ndp,
     nz,
-    send_ref,
-    take_ref,
-    image_ref,
-    owner_ref,
+    send_hbm,
+    take_hbm,
+    image_hbm,
+    owner_hbm,
     qkv_hbm,
     cot_hbm,
     w_hbm,
@@ -69,6 +69,10 @@
     gdp_recv,
     gz_send,
     gz_recv,
+    send_ref,
+    take_ref,
+    image_ref,
+    owner_ref,
     source_of,
     work_of,
     local_sem,
@@ -106,6 +110,14 @@
     qkv_copy = pltpu.make_async_copy(qkv_hbm, qkv_v, local_sem.at[0])
     cot_copy = pltpu.make_async_copy(cot_hbm, cot_v, local_sem.at[1])
     w_copy = pltpu.make_async_copy(w_hbm, wpad.at[pl.ds(64, D)], local_sem.at[2])
+    tables = [
+        pltpu.make_async_copy(source, target, local_sem.at[3 + i])
+        for i, (source, target) in enumerate(
+            ((send_hbm, send_ref), (take_hbm, take_ref), (image_hbm, image_ref), (owner_hbm, owner_ref))
+        )
+    ]
+    for copy in tables:
+        copy.start()
     qkv_copy.start()
     cot_copy.start()
 
@@ -122,6 +134,9 @@
     @pl.loop(1, NX)
     def _(i):
         pl.semaphore_signal(barrier, inc=1, device_id=(p, z * NX + x_peer(i)), device_id_type=MESH)
+
+    for copy in tables:
+        copy.wait()
 
     @pl.loop(0, nb)
     def _(v):
@@ -442,6 +457,24 @@
         pltpu.make_async_copy(gone, gone, g_send.at[which]).wait()
 
 
+def hand_over(rows_ref, grad_ref, rows_out, grad_out, rows_v, grad_v, sems):
+    inward = [
+        pltpu.make_async_copy(rows_ref, rows_v, sems.at[0]),
+        pltpu.make_async_copy(grad_ref, grad_v, sems.at[1]),
+    ]
+    outward = [
+        pltpu.make_async_copy(rows_v, rows_out, sems.at[2]),
+        pltpu.make_async_copy(grad_v, grad_out, sems.at[3]),
+    ]
+    for copy in inward:
+        copy.start()
+    for arrive, leave in zip(inward, outward):
+        arrive.wait()
+        leave.start()
+    for copy in outward:
+        copy.wait()
+
+
 def solution(mesh):
     ndp, nmp = mesh.shape["dp"], mesh.shape["mp"]
     nz = nmp // NX
@@ -451,16 +484,15 @@
     per_z = 2 * arows // nz
 
     def body(qkv, send_pos, recv_pos, block_image, owner, cotangent, out_weight):
-        smem = pl.BlockSpec(memory_space=pltpu.SMEM)
         vmem = pl.BlockSpec(memory_space=pltpu.VMEM)
-        hbm = pl.BlockSpec(memory_space=pl.ANY)
+        hbm = pl.BlockSpec(memory_space=pltpu.HBM)
         delivered, gradient = pl.pallas_call(
             functools.partial(kernel, ndp, nz),
             out_shape=(
                 jax.ShapeDtypeStruct((3 * nmp, D), BF16),
                 jax.ShapeDtypeStruct((per_z, PADDED), F32),
             ),
-            in_specs=[smem, smem, smem, vmem, hbm, hbm, hbm],
+            in_specs=[hbm] * 7,
             out_specs=(vmem, vmem),
             scratch_shapes=[
                 pltpu.VMEM((nb, BR, 3 * D), BF16),
@@ -488,7 +520,11 @@
                 pltpu.VMEM((nz, per_z, PADDED), F32),
                 pltpu.SMEM((nb,), jnp.int32),
                 pltpu.SMEM((nb,), jnp.int32),
-                pltpu.SemaphoreType.DMA((3,)),
+                pltpu.SMEM((nb,), jnp.int32),
+                pltpu.VMEM((1, rows), jnp.int32),
+                pltpu.SMEM((nb,), jnp.int32),
+                pltpu.SMEM((nb,), jnp.int32),
+                pltpu.SemaphoreType.DMA((7,)),
                 pltpu.SemaphoreType.DMA((CHUNKS,)),
                 pltpu.SemaphoreType.DMA((CHUNKS,)),
                 pltpu.SemaphoreType.DMA((CHUNKS,)),
@@ -510,6 +546,21 @@
             cotangent.reshape(nb, BR, GW),
             out_weight,
         )
+        delivered, gradient = pl.pallas_call(
+            hand_over,
+            out_shape=(
+                jax.ShapeDtypeStruct(delivered.shape, BF16),
+                jax.ShapeDtypeStruct(gradient.shape, F32),
+            ),
+            in_specs=[hbm, hbm],
+            out_specs=(hbm, hbm),
+            scratch_shapes=[
+                pltpu.VMEM(delivered.shape, BF16),
+                pltpu.VMEM(gradient.shape, F32),
+                pltpu.SemaphoreType.DMA((4,)),
+            ],
+            compiler_params=pltpu.CompilerParams(vmem_limit_bytes=62 * 2**20),
+        )(delivered, gradient)
         return delivered, gradient[:, :PIECE].reshape(-1)
 
     placed = (

time: 72.3 us -> 70.1 us (0.970)
  local copies, waits for them, and re-layouts: 3.08 us -> 0 us
  Pallas kernels: 68.3 us -> 69.3 us
    unnamed x2 -> x0, local copies, waits for them, and re-layouts: 3.08 us -> none
    pallas_call x0 -> x1, Pallas kernels: none -> 1.84 us  [body(): pl.pallas_call(hand_over, out_shape=(jax.ShapeDtypeStruct(delivered.shape...]
    pallas_call x1, Pallas kernels: 68.3 us -> 67.4 us  [body(): pl.pallas_call(functools.partial(kernel, ndp, nz), out_shape=(jax.ShapeDt...]
where the time goes in v3:
time: 70.1 us; the launch traced here: 69.9 us
  Pallas kernels  69.3 us (99%)
    pallas_call x1, Pallas kernels, body(): pl.pallas_call(functools.partial(kernel, ndp, nz), out_shape=(jax.ShapeDt...  67.4 us
    pallas_call x1, Pallas kernels, body(): pl.pallas_call(hand_over, out_shape=(jax.ShapeDtypeStruct(delivered.shape...  1.84 us

profile of v3, /device:TPU:1, one launch (start us, length us, event | category | flops | bytes accessed | tf_op | source)
XLA Modules:
  0.0 69.9 jit_solution(14763671308818176998)
XLA Ops:
  0.6 67.4 %shard_map.86 = (bf16[192,1280]{1,0:T(8,128)(2,1)}, f32[1,512]{1,0:T(1,128)}) custom-call(s32[16]{0:T(128)} %send_hbm.1, s32[16]{0:T(128)} %take_hbm.1, s32[16]{0:T(128)} %image_hbm.1, s32[1,128]{1,0:T(1,128)} %bitcast.7, bf16[16,8,3840]{2,1,0:T(8,128)(2,1)} %bitcast.5, bf16[16,8,640]{2,1,0:T(8,128)(2,1)} %bitcast.6, bf16[1280,1280]{1,0:T(8,128)(2,1)} %w_hbm.1), custom_call_target="tpu_custom_call" | custom-call | tf_op jit(solution)/shard_map/pallas_call | solution.py:489
  68.1 1.8 %shard_map.87 = (bf16[192,1280]{1,0:T(8,128)(2,1)}, f32[1,512]{1,0:T(1,128)}) custom-call(bf16[192,1280]{1,0:T(8,128)(2,1)} %get-tuple-element.6.rows_ref, f32[1,512]{1,0:T(1,128)} %get-tuple-element.7.grad_ref), custom_call_target="tpu_custom_call" | custom-call | tf_op jit(solution)/shard_map/pallas_call | solution.py:549

commit v4 on v3

--- a/solution.py
+++ b/solution.py
@@ -105,7 +105,7 @@
         return lax.rem(z + offset(i, nz), nz)
 
     def x_peer(i):
-        return lax.rem(x + i, NX)
+        return lax.rem(x + offset(i, NX), NX)
 
     qkv_copy = pltpu.make_async_copy(qkv_hbm, qkv_v, local_sem.at[0])
     cot_copy = pltpu.make_async_copy(cot_hbm, cot_v, local_sem.at[1])

time: 70.1 us -> 70.1 us (level)
  no operation moved by 1% of the time
where the time goes in v4:
time: 70.1 us; the launch traced here: 69.9 us
  Pallas kernels  69.2 us (99%)
    pallas_call x1, Pallas kernels, body(): pl.pallas_call(functools.partial(kernel, ndp, nz), out_shape=(jax.ShapeDt...  67.4 us
    pallas_call x1, Pallas kernels, body(): pl.pallas_call(hand_over, out_shape=(jax.ShapeDtypeStruct(delivered.shape...  1.84 us

profile of v4, /device:TPU:1, one launch (start us, length us, event | category | flops | bytes accessed | tf_op | source)
XLA Modules:
  0.0 69.9 jit_solution(10444461293190868503)
XLA Ops:
  0.6 67.4 %shard_map.86 = (bf16[192,1280]{1,0:T(8,128)(2,1)}, f32[1,512]{1,0:T(1,128)}) custom-call(s32[16]{0:T(128)} %send_hbm.1, s32[16]{0:T(128)} %take_hbm.1, s32[16]{0:T(128)} %image_hbm.1, s32[1,128]{1,0:T(1,128)} %bitcast.7, bf16[16,8,3840]{2,1,0:T(8,128)(2,1)} %bitcast.5, bf16[16,8,640]{2,1,0:T(8,128)(2,1)} %bitcast.6, bf16[1280,1280]{1,0:T(8,128)(2,1)} %w_hbm.1), custom_call_target="tpu_custom_call" | custom-call | tf_op jit(solution)/shard_map/pallas_call | solution.py:489
  68.0 1.8 %shard_map.87 = (bf16[192,1280]{1,0:T(8,128)(2,1)}, f32[1,512]{1,0:T(1,128)}) custom-call(bf16[192,1280]{1,0:T(8,128)(2,1)} %get-tuple-element.6.rows_ref, f32[1,512]{1,0:T(1,128)} %get-tuple-element.7.grad_ref), custom_call_target="tpu_custom_call" | custom-call | tf_op jit(solution)/shard_map/pallas_call | solution.py:549
